TPU v7x, 32 devices: a whole 2x2x4 slice. The times are simulated.
32 devices in a mesh: groups: 2 (over x), train: 8 (over z, y), query: 2 (over core).
Axes of the slice: x: 2, y: 2, z: 4, core: 2. Of those that a mesh axis runs over, the one named last changes fastest.
Arguments:
- train_grads: float32 [8192, 1024], P(('groups', 'train', 'query')), parts along dimension 0, may hold values from -60 to 60, as said below
- query_grads: float32 [2048, 1024], P(('groups', 'query'), 'train'), parts along dimension 0, may hold values from -6 to 6
Outputs:
- scores: float32 [2048, 4096], P(('groups', 'query'), 'train'), parts along dimension 0
There are 2 independent parts, one for each index of `groups`. A program takes and returns all parts, laid end to end along the dimension named above; each array names one. Nothing has to cross between parts.
Inputs may be any that keep to these rules, and one draw needn't show every extreme that they name: `train_grads`: each entry is a sum of terms of varied size, times a document scale and a coordinate scale.
All inputs are finite; a program needn't handle non-finite values.
Results may differ from a plain program's by a relative error of at most 0.0003.
Values sent between devices are 32-bit elements; how exact they have to be, the bound alone decides.
A program may use at most 128 MiB of HBM per device.

v0:
```python
import jax
import jax.numpy as jnp
from jax import lax
from jax.sharding import PartitionSpec as P


def solve_rows(lower, queries):
    middle = lax.linalg.triangular_solve(
        lower, queries, left_side=False, lower=True, transpose_a=True
    )
    return lax.linalg.triangular_solve(
        lower, middle, left_side=False, lower=True, transpose_a=False
    )


def shards(train_grads, query_grads):
    width = train_grads.shape[1]
    half = width // lax.axis_size("query")
    stacked = lax.all_gather(train_grads, "query", axis=0, tiled=True)
    own_cols = lax.dynamic_slice_in_dim(stacked, lax.axis_index("query") * half, half, 1)
    share = lax.psum_scatter(
        jnp.dot(
            stacked.T, own_cols, preferred_element_type=jnp.float32, precision=lax.Precision.HIGHEST
        ),
        "train",
        scatter_dimension=0,
        tiled=True,
    )
    tall = lax.all_gather(share, "train", axis=0, tiled=True)
    gram = lax.all_gather(tall, "query", axis=1, tiled=True)
    count_docs = lax.axis_size("train") * lax.axis_size("query") * train_grads.shape[0]
    shift = 0.1 * jnp.trace(gram) / (count_docs * width)
    curvature = gram / count_docs + shift * jnp.eye(width, dtype=jnp.float32)
    lower = jnp.linalg.cholesky(curvature)
    queries = lax.all_gather(query_grads, "train", axis=1, tiled=True)
    precond = solve_rows(lower, queries)
    scores = jnp.dot(
        precond, stacked.T, preferred_element_type=jnp.float32, precision=lax.Precision.HIGHEST
    )
    return scores / jnp.sqrt(jnp.float32(width))


def solution(mesh):
    in_specs = (P(("groups", "train", "query"), None), P(("groups", "query"), "train"))
    out_specs = P(("groups", "query"), "train")
    return jax.shard_map(shards, mesh=mesh, in_specs=in_specs, out_specs=out_specs, check_vma=False)
```

profile of v0, /device:TPU:0, one launch (start us, length us, event | category | flops | bytes accessed | tf_op | source)
XLA Modules:
  0.0 544.5 jit_solution(5021078465807214532)
XLA Ops:
  7.3 14.9 %all-gather.5.cloned.1.call-done = f32[512,1024]{1,0:T(8,128)} async-done(((f32[256,1024]{1,0:T(8,128)}), f32[512,1024]{1,0:T(8,128)}) %all-gather.5.cloned.1.call-update) | async-done | bytes 2097168 | tf_op jit(solution)/shard_map/all_gather | solution.py:19
  22.2 6.8 %convolution_bitcast_fusion = f32[1024,512]{0,1:T(8,128)} fusion(f32[512,1024]{1,0:T(8,128)} %all-gather.5.cloned.1.call-done, s32[]{:T(128)S(6)} %select_n.12), kind=kOutput, calls=%fused_computation.9 | convolution fusion | flops 3221225472 | bytes 5242884 | tf_op jit(solution)/shard_map/dot_general | solution.py:22
  29.1 69.4 %reduce-scatter.2.cloned.1.call-done = f32[128,512]{0,1:T(8,128)} async-done(((f32[1024,512]{0,1:T(8,128)}), f32[128,512]{0,1:T(8,128)}) %reduce-scatter.2.cloned.1.call-update) | async-done | bytes 262160 | tf_op jit(solution)/shard_map/reduce_scatter | solution.py:21
  98.5 52.1 %all-gather.7.cloned.1.call-done = f32[1024,512]{0,1:T(8,128)} async-done(((f32[128,512]{0,1:T(8,128)}), f32[1024,512]{0,1:T(8,128)}) %all-gather.7.cloned.1.call-update) | async-done | bytes 2097168 | tf_op jit(solution)/shard_map/all_gather | solution.py:29
  151.3 12.7 %all-gather.9.cloned.1.call-done = f32[1024,1024]{0,1:T(8,128)} async-done(((f32[1024,512]{0,1:T(8,128)}), f32[1024,1024]{0,1:T(8,128)}) %all-gather.9.cloned.1.call-update) | async-done | bytes 4194320 | tf_op jit(solution)/shard_map/all_gather | solution.py:30
  163.9 2.9 select_reduce_fusion
  167.5 5.0 select_add_fusion
  172.5 5.9 %copy.3 = f32[1024,1024]{1,0:T(8,128)} copy(f32[1024,1024]{0,1:T(8,128)} %select_add_fusion) | data formatting | bytes 8388608 | tf_op jit(solution)/shard_map/add | solution.py:33
  178.4 4.5 fusion
  184.8 11.7 %cholesky.222 = f32[128,128]{1,0:T(8,128)S(1)} custom-call(f32[128,128]{1,0:T(8,128)S(1)} %cholesky.577), custom_call_target="Cholesky" | custom-call | tf_op jit(solution)/shard_map/jit(cholesky)/cholesky | solution.py:34
  196.7 9.8 %custom-call.64 = f32[1,128,128]{1,2,0:T(8,128)S(1)} custom-call(f32[1,128,128]{2,1,0:T(8,128)S(1)} %get-tuple-element.57), custom_call_target="InvertDiagBlocksLowerTriangular" | custom-call | tf_op jit(solution)/shard_map/jit(cholesky)/cholesky | solution.py:34
  209.8 11.7 %cholesky.243 = f32[128,128]{1,0:T(8,128)S(1)} custom-call(f32[128,128]{1,0:T(8,128)S(1)} %cholesky.581), custom_call_target="Cholesky" | custom-call | tf_op jit(solution)/shard_map/jit(cholesky)/cholesky | solution.py:34
  221.8 9.8 %custom-call.65 = f32[1,128,128]{1,2,0:T(8,128)S(1)} custom-call(f32[1,128,128]{2,1,0:T(8,128)S(1)} %get-tuple-element.55), custom_call_target="InvertDiagBlocksLowerTriangular" | custom-call | tf_op jit(solution)/shard_map/jit(cholesky)/cholesky | solution.py:34
  232.7 2.0 copy-done
  234.7 2.4 convolution_subtract_fusion.1
  237.1 11.7 %cholesky.466 = f32[128,128]{1,0:T(8,128)S(1)} custom-call(f32[128,128]{1,0:T(8,128)S(1)} %cholesky.586), custom_call_target="Cholesky" | custom-call | tf_op jit(solution)/shard_map/jit(cholesky)/cholesky | solution.py:34
  249.6 9.8 %custom-call.66 = f32[1,128,128]{1,2,0:T(8,128)S(1)} custom-call(f32[1,128,128]{2,1,0:T(8,128)S(1)} %get-tuple-element.53), custom_call_target="InvertDiagBlocksLowerTriangular" | custom-call | tf_op jit(solution)/shard_map/jit(cholesky)/cholesky | solution.py:34
  260.7 3.3 convolution_subtract_fusion.2
  264.0 11.7 %cholesky.485 = f32[128,128]{1,0:T(8,128)S(1)} custom-call(f32[128,128]{1,0:T(8,128)S(1)} %cholesky.591), custom_call_target="Cholesky" | custom-call | tf_op jit(solution)/shard_map/jit(cholesky)/cholesky | solution.py:34
  276.5 9.8 %custom-call.67 = f32[1,128,128]{1,2,0:T(8,128)S(1)} custom-call(f32[1,128,128]{2,1,0:T(8,128)S(1)} %get-tuple-element.51), custom_call_target="InvertDiagBlocksLowerTriangular" | custom-call | tf_op jit(solution)/shard_map/jit(cholesky)/cholesky | solution.py:34
  287.5 3.1 convolution_subtract_fusion.17
  290.6 12.1 %cholesky.504 = f32[128,128]{1,0:T(8,128)S(1)} custom-call(f32[128,128]{1,0:T(8,128)S(1)} %cholesky.596), custom_call_target="Cholesky" | custom-call | tf_op jit(solution)/shard_map/jit(cholesky)/cholesky | solution.py:34
  303.6 9.8 %custom-call.68 = f32[1,128,128]{1,2,0:T(8,128)S(1)} custom-call(f32[1,128,128]{2,1,0:T(8,128)S(1)} %get-tuple-element.49), custom_call_target="InvertDiagBlocksLowerTriangular" | custom-call | tf_op jit(solution)/shard_map/jit(cholesky)/cholesky | solution.py:34
  314.5 3.1 convolution_subtract_fusion.18
  317.6 11.7 %cholesky.524 = f32[128,128]{1,0:T(8,128)S(1)} custom-call(f32[128,128]{1,0:T(8,128)S(1)} %cholesky.601), custom_call_target="Cholesky" | custom-call | tf_op jit(solution)/shard_map/jit(cholesky)/cholesky | solution.py:34
  330.1 9.8 %custom-call.69 = f32[1,128,128]{1,2,0:T(8,128)S(1)} custom-call(f32[1,128,128]{2,1,0:T(8,128)S(1)} %get-tuple-element.47), custom_call_target="InvertDiagBlocksLowerTriangular" | custom-call | tf_op jit(solution)/shard_map/jit(cholesky)/cholesky | solution.py:34
  340.9 2.8 convolution_subtract_fusion.19
  343.7 11.7 %cholesky.544 = f32[128,128]{1,0:T(8,128)S(1)} custom-call(f32[128,128]{1,0:T(8,128)S(1)} %cholesky.606), custom_call_target="Cholesky" | custom-call | tf_op jit(solution)/shard_map/jit(cholesky)/cholesky | solution.py:34
  356.2 9.8 %custom-call.70 = f32[1,128,128]{1,2,0:T(8,128)S(1)} custom-call(f32[1,128,128]{2,1,0:T(8,128)S(1)} %get-tuple-element.45), custom_call_target="InvertDiagBlocksLowerTriangular" | custom-call | tf_op jit(solution)/shard_map/jit(cholesky)/cholesky | solution.py:34
  367.0 2.1 convolution_subtract_fusion.20
  369.1 11.7 %cholesky.562 = f32[128,128]{1,0:T(8,128)S(1)} custom-call(f32[128,128]{1,0:T(8,128)S(1)} %convolution_subtract_fusion.20), custom_call_target="Cholesky" | custom-call | tf_op jit(solution)/shard_map/jit(cholesky)/cholesky | solution.py:34
  391.3 4.8 select_select_fusion
  396.1 23.7 %while.1 = (s32[]{:T(128)}, f32[1024,1024]{0,1:T(8,128)}, s32[8,2]{0,1:T(2,128)S(1)}, f32[8,128,128]{2,1,0:T(8,128)S(1)}, s32[]{:T(128)}) while((s32[]{:T(128)}, f32[1024,1024]{0,1:T(8,128)}, s32[8,2]{0,1:T(2,128)S(1)}, f32[8,128,128]{2,1,0:T(8,128)S(1)}, s32[]{:T(128)}) %tuple.49), condition=%wide.while_cond, body=%wide.while_body.sunk | while | flops 2 | bytes 393329 | solution.py:8
  396.7 2.2 dynamic-slice.7
  399.7 2.2 dynamic-slice.7
  402.7 2.2 dynamic-slice.7
  405.7 2.2 dynamic-slice.7
  408.6 2.2 dynamic-slice.7
  411.6 2.2 dynamic-slice.7
  414.6 2.2 dynamic-slice.7
  417.6 2.2 dynamic-slice.7
  419.9 79.0 %custom-call.71 = f32[8,128,128]{1,2,0:T(8,128)S(1)} custom-call(f32[8,128,128]{2,1,0:T(8,128)S(1)} %get-tuple-element.12), custom_call_target="InvertDiagBlocksLowerTriangular" | custom-call | tf_op jit(solution)/shard_map/triangular_solve | solution.py:8
  502.5 2.0 convolution_subtract_fusion.9
  505.0 2.6 convolution_subtract_fusion.14
  510.3 2.3 convolution_subtract_fusion.8
  513.0 2.6 convolution_subtract_fusion.13
  516.2 3.1 convolution_subtract_fusion.7
  529.9 7.9 %convolution_multiply_fusion = f32[512,512]{1,0:T(8,128)} fusion(f32[512,1024]{0,1:T(8,128)S(1)} %constant_dynamic-update-slice_fusion.36, f32[512,1024]{1,0:T(8,128)S(1)} %copy-done.3), kind=kOutput, calls=%fused_computation.10 | convolution fusion | flops 3221487616 | bytes 5242880 | tf_op jit(solution)/shard_map/dot_general | solution.py:37
  (150 shorter events, 46.8 us)
Async XLA Ops:
  6.5 15.7 %all-gather.5.cloned.1.call-start = ((), (), s32[]{:S(2)}) async-start(), calls=%async_computation.1 | async-start | bytes 3145728 | tf_op jit(solution)/shard_map/all_gather | solution.py:19
  7.3 91.2 %reduce-scatter.2.cloned.1.call-start = ((), (), s32[]{:S(2)}) async-start(), calls=%async_computation.2 | async-start | bytes 2359296 | tf_op jit(solution)/shard_map/reduce_scatter | solution.py:21
  29.0 121.6 %all-gather.7.cloned.1.call-start = ((), (), s32[]{:S(2)}) async-start(), calls=%async_computation.3 | async-start | bytes 2359296 | tf_op jit(solution)/shard_map/all_gather | solution.py:29
  98.5 65.4 %all-gather.9.cloned.1.call-start = ((), (), s32[]{:S(2)}) async-start(), calls=%async_computation.4 | async-start | bytes 6291456 | tf_op jit(solution)/shard_map/all_gather | solution.py:30
  150.7 348.2 %all-gather.11.cloned.1.call-start = ((), (), s32[]{:S(2)}) async-start(), calls=%async_computation.5 | async-start | bytes 2359296 | tf_op jit(solution)/shard_map/all_gather | solution.py:35
  182.9 1.9 copy-start.2
  232.7 2.0 copy-start
  500.3 4.7 copy-start.1
  504.5 3.5 copy-start.4
  528.3 1.6 copy-start.3
Sparse Core Ops, SparseCore 0:
  8.9 13.2 all-gather.4
  29.2 69.2 reduce-scatter.1
  100.5 50.0 all-gather.6
  152.0 11.8 all-gather.8
  165.8 52.4 all-gather.10
where the time goes:
time: 549 us; the launch traced here: 545 us
  other arithmetic  264 us (48%)
  waiting for transfers between devices  150 us (27%)
  matrix products  69.7 us (13%)
  local copies, waits for them, and re-layouts  40.2 us (7%)
  between operations  19.7 us (4%)
    another operation x30, other arithmetic, shards(): lower = jnp.linalg.cholesky(curvature)  168 us
    another operation x3, other arithmetic, solve_rows(): lax.linalg.triangular_solve(lower, queries, left_side=False, lower=True,...  83.8 us
    reduce_scatter x1, waiting for transfers between devices, shards(): lax.psum_scatter(jnp.dot(stacked.T, own_cols, preferred_element_type=jnp....  69.4 us
    all_gather x1, waiting for transfers between devices, shards(): tall = lax.all_gather(share, 'train', axis=0, tiled=True)  52.1 us
    another operation x14, matrix products, shards(): lower = jnp.linalg.cholesky(curvature)  25.9 us
    another operation x40, local copies, waits for them, and re-layouts  23.5 us
    another operation x15, matrix products, solve_rows(): lax.linalg.triangular_solve(lower, queries, left_side=False, lower=True,...  20.6 us
    all_gather x1, waiting for transfers between devices, shards(): stacked = lax.all_gather(train_grads, 'query', axis=0, tiled=True)  14.9 us
  transfers between devices with their start and end apart: 5, of which 4 were waited for; matrix products, arithmetic and copies ran while one was open for 60% of the time, Pallas kernels for 0%

commit v1 on v0

v1 whole, which is shorter than its diff:
```python
import functools

import jax
import jax.numpy as jnp
from jax import lax
from jax.experimental import pallas as pl
from jax.experimental.pallas import tpu as pltpu
from jax.sharding import PartitionSpec as P

HIGHEST = lax.Precision.HIGHEST
SIDE = 128
ROWS = 8


def dot(a, b, dims=((1,), (0,))):
    return lax.dot_general(
        a, b, (dims, ((), ())), precision=HIGHEST, preferred_element_type=jnp.float32
    )


def invert_small(cols, row):
    for s in range(ROWS):
        inv = 1.0 / jnp.broadcast_to(cols[s][s : s + 1], cols[s].shape)
        here = row == s
        pivot = cols[s]
        out = []
        for j in range(ROWS):
            if j == s:
                out.append(jnp.where(here, inv, -pivot * inv))
            else:
                r = jnp.broadcast_to(cols[j][s : s + 1], pivot.shape) * inv
                out.append(jnp.where(here, r, cols[j] - pivot * r))
        cols = out
    return cols


def spread(block, lane):
    return jnp.take_along_axis(block, jnp.full(block.shape, lane, jnp.int32), axis=1)


def invert_block(d_ref):
    panels = SIDE // ROWS
    row = lax.broadcasted_iota(jnp.int32, (ROWS, SIDE), 0)
    lane = lax.broadcasted_iota(jnp.int32, (ROWS, SIDE), 1)

    def step(g, carry):
        base = g * ROWS
        at = pl.ds(pl.multiple_of(base, ROWS), ROWS)
        own = d_ref[at, :]
        cols = invert_small([spread(own, base + s) for s in range(ROWS)], row)
        inside = (lane >= base) & (lane < base + ROWS)
        start = jnp.where(inside, jnp.where(lane - base == row, 1.0, 0.0), own)
        fresh = cols[0] * jnp.broadcast_to(start[0:1], start.shape)
        for s in range(1, ROWS):
            fresh = fresh + cols[s] * jnp.broadcast_to(start[s : s + 1], start.shape)
        wide = [jnp.broadcast_to(fresh[s : s + 1], fresh.shape) for s in range(ROWS)]
        for i in range(panels):
            block = d_ref[i * ROWS : (i + 1) * ROWS, :]
            new = jnp.where(inside, 0.0, block)
            for s in range(ROWS):
                new = new - spread(block, base + s) * wide[s]
            d_ref[i * ROWS : (i + 1) * ROWS, :] = new
        d_ref[at, :] = fresh
        return carry

    lax.fori_loop(0, panels, step, 0)


def solve_kernel(gram_ref, query_ref, out_ref, a_ref, inv_ref):
    width = gram_ref.shape[0]
    count = width // SIDE
    eye = lax.broadcasted_iota(jnp.int32, (SIDE, SIDE), 0) == lax.broadcasted_iota(
        jnp.int32, (SIDE, SIDE), 1
    )
    span = [slice(k * SIDE, (k + 1) * SIDE) for k in range(count)]
    diag = jnp.zeros((SIDE, SIDE), jnp.float32)
    for k in range(count):
        diag = diag + jnp.where(eye, gram_ref[span[k], span[k]], 0.0)
    shift = 0.1 * jnp.sum(diag) / width
    for k in range(count):
        a_ref[span[k], k * SIDE :] = gram_ref[span[k], k * SIDE :]
        a_ref[span[k], span[k]] += jnp.where(eye, shift, 0.0)
    out_ref[...] = query_ref[...]
    for k in range(count):
        inv_ref[k] = a_ref[span[k], span[k]]
        invert_block(inv_ref.at[k])
        if k + 1 == count:
            break
        rest = a_ref[span[k], (k + 1) * SIDE :]
        w = dot(inv_ref[k], rest)
        for i in range(k + 1, count):
            off = (i - k - 1) * SIDE
            a_ref[span[i], i * SIDE :] -= dot(
                rest[:, off : off + SIDE], w[:, off:], ((0,), (0,))
            )
        a_ref[span[k], (k + 1) * SIDE :] = w
        out_ref[:, (k + 1) * SIDE :] -= dot(out_ref[:, span[k]], w)
    for k in reversed(range(count)):
        z = dot(out_ref[:, span[k]], inv_ref[k])
        if k + 1 < count:
            z = z - dot(
                out_ref[:, (k + 1) * SIDE :], a_ref[span[k], (k + 1) * SIDE :], ((1,), (1,))
            )
        out_ref[:, span[k]] = z


def solve_rows(gram, queries):
    width = gram.shape[0]
    vmem = pl.BlockSpec(memory_space=pltpu.VMEM)
    return pl.pallas_call(
        solve_kernel,
        out_shape=jax.ShapeDtypeStruct(queries.shape, jnp.float32),
        in_specs=[vmem, vmem],
        out_specs=vmem,
        scratch_shapes=[
            pltpu.VMEM((width, width), jnp.float32),
            pltpu.VMEM((width // SIDE, SIDE, SIDE), jnp.float32),
        ],
        compiler_params=pltpu.CompilerParams(vmem_limit_bytes=48 * 2**20),
    )(gram, queries)


def shards(train_grads, query_grads):
    width = train_grads.shape[1]
    half = width // lax.axis_size("query")
    stacked = lax.all_gather(train_grads, "query", axis=0, tiled=True)
    own_cols = lax.dynamic_slice_in_dim(stacked, lax.axis_index("query") * half, half, 1)
    share = lax.psum_scatter(
        jnp.dot(stacked.T, own_cols, preferred_element_type=jnp.float32, precision=HIGHEST),
        "train",
        scatter_dimension=0,
        tiled=True,
    )
    tall = lax.all_gather(share, "train", axis=0, tiled=True)
    gram = lax.all_gather(tall, "query", axis=1, tiled=True)
    count_docs = lax.axis_size("train") * lax.axis_size("query") * train_grads.shape[0]
    queries = lax.all_gather(query_grads, "train", axis=1, tiled=True)
    precond = solve_rows(gram, queries)
    scores = jnp.dot(precond, stacked.T, preferred_element_type=jnp.float32, precision=HIGHEST)
    return scores * (count_docs / jnp.sqrt(jnp.float32(width)))


def solution(mesh):
    in_specs = (P(("groups", "train", "query"), None), P(("groups", "query"), "train"))
    out_specs = P(("groups", "query"), "train")
    return jax.shard_map(shards, mesh=mesh, in_specs=in_specs, out_specs=out_specs, check_vma=False)
```

time: 549 us -> 312 us (0.57)
  other arithmetic: 264 us -> 0 us
  Pallas kernels: 0 us -> 85.8 us
  matrix products: 69.7 us -> 11.2 us
  waiting for transfers between devices: 150 us -> 200 us
  local copies, waits for them, and re-layouts: 40.2 us -> 1.59 us
  between operations: 19.7 us -> 13.2 us
    another operation x33 -> x0, other arithmetic: 252 us -> none  [the longest x30 168 us: shards(): lower = jnp.linalg.cholesky(curvature)]
    pallas_call x0 -> x1, Pallas kernels: none -> 85.8 us  [solve_rows(): pl.pallas_call(solve_kernel, out_shape=jax.ShapeDtypeStruct(queries.shape...]
    another operation x44 -> x0, matrix products: 55 us -> none  [the longest x14 25.9 us: shards(): lower = jnp.linalg.cholesky(curvature)]
    all_gather x1, waiting for transfers between devices: 0.02 us -> 51.5 us  [shards(): queries = lax.all_gather(query_grads, 'train', axis=1, tiled=True)]
    another operation x70 -> x0, local copies, waits for them, and re-layouts: 29.1 us -> none
    add x1 -> x0, local copies, waits for them, and re-layouts: 5.88 us -> none  [shards(): curvature = gram / count_docs + shift * jnp.eye(width, dtype=jnp.float32)]
  transfers between devices with their start and end apart: 5 -> 5, of which waited for: 4 -> 5; matrix products, arithmetic and copies ran while one was open for 60% -> 0% of each run, Pallas kernels for 0% -> 0%
where the time goes in v1:
time: 312 us
  waiting for transfers between devices  200 us (64%)
  Pallas kernels  85.8 us (28%)
  between operations  13.2 us (4%)
  matrix products  11.2 us (4%)
    pallas_call x1, Pallas kernels, solve_rows(): pl.pallas_call(solve_kernel, out_shape=jax.ShapeDtypeStruct(queries.shape...  85.8 us
    reduce_scatter x1, waiting for transfers between devices, shards(): lax.psum_scatter(jnp.dot(stacked.T, own_cols, preferred_element_type=jnp....  69.1 us
    all_gather x1, waiting for transfers between devices, shards(): queries = lax.all_gather(query_grads, 'train', axis=1, tiled=True)  51.5 us
    all_gather x1, waiting for transfers between devices, shards(): tall = lax.all_gather(share, 'train', axis=0, tiled=True)  49.9 us
    all_gather x1, waiting for transfers between devices, shards(): stacked = lax.all_gather(train_grads, 'query', axis=0, tiled=True)  14.9 us
    all_gather x1, waiting for transfers between devices, shards(): gram = lax.all_gather(tall, 'query', axis=1, tiled=True)  13.3 us
    dot_general x1, matrix products, shards(): jnp.dot(stacked.T, own_cols, preferred_element_type=jnp.float32, precisio...  6.74 us
  transfers between devices with their start and end apart: 5, of which 5 were waited for; matrix products, arithmetic and copies ran while one was open for 0% of the time, Pallas kernels for 0%

profile of v1, /device:TPU:0, one launch (start us, length us, event | category | flops | bytes accessed | tf_op | source)
XLA Modules:
  0.0 311.8 jit_solution(16001666293712067951)
XLA Ops:
  6.5 0.0 all-gather.5.cloned.1.call-start
  6.5 0.7 all-gather.5.cloned.1.call-update
  7.3 0.0 reduce-scatter.2.cloned.1.call-start
  7.3 14.9 %all-gather.5.cloned.1.call-done = f32[512,1024]{1,0:T(8,128)} async-done(((f32[256,1024]{1,0:T(8,128)}), f32[512,1024]{1,0:T(8,128)}) %all-gather.5.cloned.1.call-update) | async-done | bytes 2097168 | tf_op jit(solution)/shard_map/all_gather | solution.py:126
  22.2 6.7 %convolution_bitcast_fusion = f32[1024,512]{1,0:T(8,128)} fusion(f32[512,1024]{1,0:T(8,128)} %all-gather.5.cloned.1.call-done, s32[]{:T(128)S(6)} %select_n.3), kind=kOutput, calls=%fused_computation | convolution fusion | flops 3221225472 | bytes 5242884 | tf_op jit(solution)/shard_map/dot_general | solution.py:129
  28.9 0.0 reduce-scatter.2.cloned.1.call-update
  29.0 0.0 all-gather.7.cloned.1.call-start
  29.0 69.1 %reduce-scatter.2.cloned.1.call-done = f32[128,512]{1,0:T(8,128)} async-done(((f32[1024,512]{1,0:T(8,128)}), f32[128,512]{1,0:T(8,128)}) %reduce-scatter.2.cloned.1.call-update) | async-done | bytes 262160 | tf_op jit(solution)/shard_map/reduce_scatter | solution.py:128
  98.1 0.0 all-gather.7.cloned.1.call-update
  98.1 0.0 all-gather.11.cloned.1.call-start
  98.2 0.5 all-gather.11.cloned.1.call-update
  98.7 0.0 all-gather.9.cloned.1.call-start
  98.7 49.9 %all-gather.7.cloned.1.call-done = f32[1024,512]{1,0:T(8,128)} async-done(((f32[128,512]{1,0:T(8,128)}), f32[1024,512]{1,0:T(8,128)}) %all-gather.7.cloned.1.call-update) | async-done | bytes 2097168 | tf_op jit(solution)/shard_map/all_gather | solution.py:134
  148.6 0.0 copy-start.1
  148.6 0.0 all-gather.9.cloned.1.call-update
  148.6 51.5 %all-gather.11.cloned.1.call-done.query_ref = f32[512,1024]{1,0:T(8,128)} async-done(((f32[512,128]{1,0:T(8,128)}), f32[512,1024]{1,0:T(8,128)}) %all-gather.11.cloned.1.call-update) | async-done | bytes 2097168 | tf_op jit(solution)/shard_map/all_gather | solution.py:137
  200.1 13.3 %all-gather.9.cloned.1.call-done.gram_ref = f32[1024,1024]{1,0:T(8,128)} async-done(((f32[1024,512]{1,0:T(8,128)}), f32[1024,1024]{1,0:T(8,128)}) %all-gather.9.cloned.1.call-update) | async-done | bytes 4194320 | tf_op jit(solution)/shard_map/all_gather | solution.py:135
  213.4 0.0 copy-start
  213.4 1.6 copy-done
  215.0 85.8 %shard_map.28 = f32[512,1024]{1,0:T(8,128)S(1)} custom-call(f32[1024,1024]{1,0:T(8,128)} %all-gather.9.cloned.1.call-done.gram_ref, f32[512,1024]{1,0:T(8,128)S(1)} %copy-done), custom_call_target="tpu_custom_call" | custom-call | tf_op jit(solution)/shard_map/pallas_call | solution.py:110
  300.8 0.0 copy-done.1
  300.8 4.5 %convolution_multiply_fusion = f32[512,512]{1,0:T(8,128)} fusion(f32[512,1024]{1,0:T(8,128)S(1)} %shard_map.28, f32[512,1024]{1,0:T(8,128)S(1)} %copy-done.1), kind=kOutput, calls=%fused_computation.1 | convolution fusion | flops 3221487616 | bytes 5242880 | tf_op jit(solution)/shard_map/dot_general | solution.py:139
Async XLA Ops:
  6.5 15.7 %all-gather.5.cloned.1.call-start = ((), (), s32[]{:S(2)}) async-start(), calls=%async_computation.1 | async-start | bytes 3145728 | tf_op jit(solution)/shard_map/all_gather | solution.py:126
  7.3 90.8 %reduce-scatter.2.cloned.1.call-start = ((), (), s32[]{:S(2)}) async-start(), calls=%async_computation.2 | async-start | bytes 2359296 | tf_op jit(solution)/shard_map/reduce_scatter | solution.py:128
  29.0 119.6 %all-gather.7.cloned.1.call-start = ((), (), s32[]{:S(2)}) async-start(), calls=%async_computation.3 | async-start | bytes 2359296 | tf_op jit(solution)/shard_map/all_gather | solution.py:134
  98.1 102.0 %all-gather.11.cloned.1.call-start = ((), (), s32[]{:S(2)}) async-start(), calls=%async_computation.5 | async-start | bytes 2359296 | tf_op jit(solution)/shard_map/all_gather | solution.py:137
  98.7 114.7 %all-gather.9.cloned.1.call-start = ((), (), s32[]{:S(2)}) async-start(), calls=%async_computation.4 | async-start | bytes 6291456 | tf_op jit(solution)/shard_map/all_gather | solution.py:135
  148.6 152.2 %copy-start.1 = (f32[512,1024]{1,0:T(8,128)S(1)}, f32[512,1024]{1,0:T(8,128)}, u32[]{:S(2)}) copy-start(f32[512,1024]{1,0:T(8,128)} %all-gather.5.cloned.1.call-done) | copy-start | bytes 6291460
  213.4 1.6 copy-start
Sparse Core Ops, SparseCore 0:
  8.9 13.2 all-gather.4
  29.1 68.9 reduce-scatter.1
  100.2 48.3 all-gather.6
  150.5 49.5 all-gather.10
  201.5 11.8 all-gather.8

commit v2 on v1

--- a/solution.py
+++ b/solution.py
@@ -66,8 +66,132 @@
     lax.fori_loop(0, panels, step, 0)
 
 
-def solve_kernel(gram_ref, query_ref, out_ref, a_ref, inv_ref):
-    width = gram_ref.shape[0]
+def band_width(width):
+    return width // 2 + SIDE
+
+
+def gram_kernel(teams, own_ref, stacked_ref, band_ref, turned, part, slots, sems, pair_sem):
+    docs, width = own_ref.shape
+    half, wide = width // 2, band_width(width)
+    rows = half // teams
+    t, c = lax.axis_index("train"), lax.axis_index("query")
+    other = 1 - c
+
+    def mine(team, core):
+        return pl.ds(pl.multiple_of(core * half + team * rows, rows), rows)
+
+    def away(d):
+        return lax.rem(t + d, teams), lax.rem(t + teams - d, teams)
+
+    def push(src, dst, send, recv, team, core):
+        return pltpu.make_async_remote_copy(
+            src_ref=src,
+            dst_ref=dst,
+            send_sem=send,
+            recv_sem=recv,
+            device_id={"train": team, "query": core},
+            device_id_type=pl.DeviceIdType.MESH,
+        )
+
+    barrier = pltpu.get_barrier_semaphore()
+    for d in range(1, teams):
+        pl.semaphore_signal(
+            barrier, inc=1, device_id={"train": away(d)[0], "query": c},
+            device_id_type=pl.DeviceIdType.MESH,
+        )
+    pl.semaphore_signal(
+        barrier, inc=1, device_id={"train": t, "query": other},
+        device_id_type=pl.DeviceIdType.MESH,
+    )
+    pl.semaphore_wait(barrier, teams)
+
+    def docs_of(core):
+        return pl.ds(pl.multiple_of(core * docs, docs), docs)
+
+    pair = push(own_ref, stacked_ref.at[docs_of(c), :], pair_sem.at[0], pair_sem.at[1], t, other)
+    pair.start()
+    stacked_ref[docs_of(c), :] = own_ref[...]
+    pair.wait()
+    turned[:, :half] = stacked_ref[:, pl.ds(pl.multiple_of(c * half, half), half)]
+    turned[:, half:] = stacked_ref[:, pl.ds(pl.multiple_of(other * half, half), half)]
+    for i in range(half // SIDE):
+        lo = i * SIDE
+        part[lo : lo + SIDE, :] = dot(
+            turned[:, lo : lo + SIDE], turned[:, lo : lo + wide], ((0,), (0,))
+        )
+
+    def shares(d):
+        to, _ = away(d)
+        return push(
+            part.at[pl.ds(pl.multiple_of(to * rows, rows), rows), :],
+            slots.at[d], sems.at[0, d], sems.at[1, d], to, c,
+        )
+
+    for d in range(1, teams):
+        shares(d).start()
+    total = part[pl.ds(pl.multiple_of(t * rows, rows), rows), :]
+    for d in range(1, teams):
+        shares(d).wait_recv()
+        total = total + slots[d]
+    band_ref[mine(t, c), :] = total
+
+    def spreads(d):
+        return push(
+            band_ref.at[mine(t, c), :], band_ref.at[mine(t, c), :],
+            sems.at[2, d], sems.at[3, d], away(d)[0], c,
+        )
+
+    def relays(d):
+        owner = away(d)[1]
+        return push(
+            band_ref.at[mine(owner, c), :], band_ref.at[mine(owner, c), :],
+            sems.at[4, d], sems.at[5, d], t, other,
+        )
+
+    for d in range(1, teams):
+        spreads(d).start()
+    relays(0).start()
+    for d in range(1, teams):
+        spreads(d).wait_recv()
+        relays(d).start()
+    for d in range(teams):
+        relays(d).wait_recv()
+    for d in range(1, teams):
+        shares(d).wait_send()
+        spreads(d).wait_send()
+    for d in range(teams):
+        relays(d).wait_send()
+
+
+def gram_band(train_grads):
+    teams = lax.axis_size("train")
+    docs, width = train_grads.shape
+    wide = band_width(width)
+    rows = width // (2 * teams)
+    vmem = pl.BlockSpec(memory_space=pltpu.VMEM)
+    return pl.pallas_call(
+        functools.partial(gram_kernel, teams),
+        out_shape=[
+            jax.ShapeDtypeStruct((2 * docs, width), jnp.float32),
+            jax.ShapeDtypeStruct((width, wide), jnp.float32),
+        ],
+        in_specs=[vmem],
+        out_specs=[vmem, vmem],
+        scratch_shapes=[
+            pltpu.VMEM((2 * docs, width), jnp.float32),
+            pltpu.VMEM((width // 2, wide), jnp.float32),
+            pltpu.VMEM((teams, rows, wide), jnp.float32),
+            pltpu.SemaphoreType.DMA((6, teams)),
+            pltpu.SemaphoreType.DMA((2,)),
+        ],
+        compiler_params=pltpu.CompilerParams(
+            vmem_limit_bytes=48 * 2**20, collective_id=0, has_side_effects=True
+        ),
+    )(train_grads)
+
+
+def factor_kernel(band_ref, a_ref, inv_ref):
+    width = band_ref.shape[0]
     count = width // SIDE
     eye = lax.broadcasted_iota(jnp.int32, (SIDE, SIDE), 0) == lax.broadcasted_iota(
         jnp.int32, (SIDE, SIDE), 1
@@ -75,12 +199,18 @@
     span = [slice(k * SIDE, (k + 1) * SIDE) for k in range(count)]
     diag = jnp.zeros((SIDE, SIDE), jnp.float32)
     for k in range(count):
-        diag = diag + jnp.where(eye, gram_ref[span[k], span[k]], 0.0)
+        diag = diag + jnp.where(eye, band_ref[span[k], span[0]], 0.0)
     shift = 0.1 * jnp.sum(diag) / width
-    for k in range(count):
-        a_ref[span[k], k * SIDE :] = gram_ref[span[k], k * SIDE :]
-        a_ref[span[k], span[k]] += jnp.where(eye, shift, 0.0)
-    out_ref[...] = query_ref[...]
+    for i in range(count):
+        for d in range(count // 2 + 1):
+            block = band_ref[span[i], span[d]]
+            j = (i + d) % count
+            if d == 0:
+                a_ref[span[i], span[i]] = block + jnp.where(eye, shift, 0.0)
+            elif j > i:
+                a_ref[span[i], span[j]] = block
+            elif 2 * d < count:
+                a_ref[span[j], span[i]] = block.T
     for k in range(count):
         inv_ref[k] = a_ref[span[k], span[k]]
         invert_block(inv_ref.at[k])
@@ -94,7 +224,16 @@
                 rest[:, off : off + SIDE], w[:, off:], ((0,), (0,))
             )
         a_ref[span[k], (k + 1) * SIDE :] = w
-        out_ref[:, (k + 1) * SIDE :] -= dot(out_ref[:, span[k]], w)
+
+
+def solve_kernel(a_ref, inv_ref, query_ref, out_ref):
+    count = inv_ref.shape[0]
+    span = [slice(k * SIDE, (k + 1) * SIDE) for k in range(count)]
+    out_ref[...] = query_ref[...]
+    for k in range(count - 1):
+        out_ref[:, (k + 1) * SIDE :] -= dot(
+            out_ref[:, span[k]], a_ref[span[k], (k + 1) * SIDE :]
+        )
     for k in reversed(range(count)):
         z = dot(out_ref[:, span[k]], inv_ref[k])
         if k + 1 < count:
@@ -104,38 +243,43 @@
         out_ref[:, span[k]] = z
 
 
-def solve_rows(gram, queries):
-    width = gram.shape[0]
+def factor(band):
+    width = band.shape[0]
+    vmem = pl.BlockSpec(memory_space=pltpu.VMEM)
+    return pl.pallas_call(
+        factor_kernel,
+        out_shape=[
+            jax.ShapeDtypeStruct((width, width), jnp.float32),
+            jax.ShapeDtypeStruct((width // SIDE, SIDE, SIDE), jnp.float32),
+        ],
+        in_specs=[vmem],
+        out_specs=[vmem, vmem],
+        compiler_params=pltpu.CompilerParams(vmem_limit_bytes=48 * 2**20),
+        cost_estimate=pl.CostEstimate(
+            flops=12 * width**3, bytes_accessed=256 * 2**20, transcendentals=0
+        ),
+    )(band)
+
+
+def solve_rows(upper, inverses, queries):
     vmem = pl.BlockSpec(memory_space=pltpu.VMEM)
     return pl.pallas_call(
         solve_kernel,
         out_shape=jax.ShapeDtypeStruct(queries.shape, jnp.float32),
-        in_specs=[vmem, vmem],
+        in_specs=[vmem, vmem, vmem],
         out_specs=vmem,
-        scratch_shapes=[
-            pltpu.VMEM((width, width), jnp.float32),
-            pltpu.VMEM((width // SIDE, SIDE, SIDE), jnp.float32),
-        ],
         compiler_params=pltpu.CompilerParams(vmem_limit_bytes=48 * 2**20),
-    )(gram, queries)
+    )(upper, inverses, queries)
 
 
 def shards(train_grads, query_grads):
     width = train_grads.shape[1]
-    half = width // lax.axis_size("query")
-    stacked = lax.all_gather(train_grads, "query", axis=0, tiled=True)
-    own_cols = lax.dynamic_slice_in_dim(stacked, lax.axis_index("query") * half, half, 1)
-    share = lax.psum_scatter(
-        jnp.dot(stacked.T, own_cols, preferred_element_type=jnp.float32, precision=HIGHEST),
-        "train",
-        scatter_dimension=0,
-        tiled=True,
-    )
-    tall = lax.all_gather(share, "train", axis=0, tiled=True)
-    gram = lax.all_gather(tall, "query", axis=1, tiled=True)
     count_docs = lax.axis_size("train") * lax.axis_size("query") * train_grads.shape[0]
+    stacked, band = gram_band(train_grads)
+    band, query_grads = lax.optimization_barrier((band, query_grads))
     queries = lax.all_gather(query_grads, "train", axis=1, tiled=True)
-    precond = solve_rows(gram, queries)
+    upper, inverses = factor(band)
+    precond = solve_rows(upper, inverses, queries)
     scores = jnp.dot(precond, stacked.T, preferred_element_type=jnp.float32, precision=HIGHEST)
     return scores * (count_docs / jnp.sqrt(jnp.float32(width)))
 

time: 312 us -> 184 us (0.59)
  the two profiles are of different devices: /device:TPU:0 before, /device:TPU:29 now
where the time goes in v2:
time: 184 us
  Pallas kernels  160 us (87%)
  between operations  13.4 us (7%)
  local copies, waits for them, and re-layouts  6.06 us (3%)
  matrix products  4.5 us (2%)
    pallas_call x1, Pallas kernels, gram_band(): pl.pallas_call(functools.partial(gram_kernel, teams), out_shape=[jax.Shap...  73.7 us
    pallas_call x1, Pallas kernels, factor(): pl.pallas_call(factor_kernel, out_shape=[jax.ShapeDtypeStruct((width, wid...  66.5 us
    pallas_call x1, Pallas kernels, solve_rows(): pl.pallas_call(solve_kernel, out_shape=jax.ShapeDtypeStruct(queries.shape...  19.9 us
    unnamed x8, local copies, waits for them, and re-layouts  6.06 us
    dot_general x1, matrix products, shards(): jnp.dot(precond, stacked.T, preferred_element_type=jnp.float32, precision...  4.5 us
  transfers between devices with their start and end apart: 1, of which 0 were waited for; matrix products, arithmetic and copies ran while one was open for 0% of the time, Pallas kernels for 36%

profile of v2, /device:TPU:29, one launch (start us, length us, event | category | flops | bytes accessed | tf_op | source)
XLA Modules:
  0.0 184.1 jit_solution(5025543454437723674)
XLA Ops:
  6.5 0.0 all-gather.2.cloned.1.call-start
  6.5 0.0 copy-start.1
  6.5 1.2 copy-done.1
  7.8 73.7 %shard_map.28 = (f32[512,1024]{1,0:T(8,128)S(1)}, f32[1024,640]{1,0:T(8,128)S(1)}) custom-call(f32[256,1024]{1,0:T(8,128)S(1)} %copy-done.1), custom_call_target="tpu_custom_call" | custom-call | tf_op jit(solution)/shard_map/pallas_call | solution.py:172
  81.4 0.0 copy-start.2
  81.4 1.5 copy-done.2
  83.0 0.0 all-gather.2.cloned.1.call-update
  83.0 0.0 copy-start.3
  83.0 1.7 copy-done.3
  84.7 66.5 %shard_map.29 = (f32[1024,1024]{1,0:T(8,128)}, f32[8,128,128]{2,1,0:T(8,128)S(1)}) custom-call(f32[1024,640]{1,0:T(8,128)S(1)} %copy-done.3), custom_call_target="tpu_custom_call" | custom-call | flops 12884901888 | bytes 268435456 | tf_op jit(solution)/shard_map/pallas_call | solution.py:249
  151.2 0.0 all-gather.2.cloned.1.call-done.query_ref
  151.2 0.0 copy-start
  151.2 1.6 copy-done
  152.8 19.9 %shard_map.30 = f32[512,1024]{1,0:T(8,128)S(1)} custom-call(f32[1024,1024]{1,0:T(8,128)} %get-tuple-element.13.a_ref, f32[8,128,128]{2,1,0:T(8,128)S(1)} %get-tuple-element.14.inv_ref, f32[512,1024]{1,0:T(8,128)S(1)} %copy-done), custom_call_target="tpu_custom_call" | custom-call | tf_op jit(solution)/shard_map/pallas_call | solution.py:266
  172.7 4.5 %convolution_multiply_fusion = f32[512,512]{1,0:T(8,128)} fusion(f32[512,1024]{1,0:T(8,128)S(1)} %shard_map.30, f32[512,1024]{1,0:T(8,128)S(1)} %get-tuple-element.16), kind=kOutput, calls=%fused_computation | convolution fusion | flops 3221487616 | bytes 5242880 | tf_op jit(solution)/shard_map/dot_general | solution.py:283
Async XLA Ops:
  6.5 144.7 %all-gather.2.cloned.1.call-start = ((), (), s32[]{:S(2)}) async-start(), calls=%async_computation | async-start | bytes 2359296 | tf_op jit(solution)/shard_map/all_gather | solution.py:280
  6.5 1.2 copy-start.1
  81.4 1.5 copy-start.2
  83.0 1.7 copy-start.3
  151.2 1.6 copy-start
Sparse Core Ops, SparseCore 0:
  83.1 48.8 all-gather.1

commit v3 on v2

--- a/solution.py
+++ b/solution.py
@@ -38,12 +38,12 @@
     return jnp.take_along_axis(block, jnp.full(block.shape, lane, jnp.int32), axis=1)
 
 
-def invert_block(d_ref):
+def invert_block(d_ref, beside=None):
     panels = SIDE // ROWS
     row = lax.broadcasted_iota(jnp.int32, (ROWS, SIDE), 0)
     lane = lax.broadcasted_iota(jnp.int32, (ROWS, SIDE), 1)
 
-    def step(g, carry):
+    def panel(g):
         base = g * ROWS
         at = pl.ds(pl.multiple_of(base, ROWS), ROWS)
         own = d_ref[at, :]
@@ -61,9 +61,15 @@
                 new = new - spread(block, base + s) * wide[s]
             d_ref[i * ROWS : (i + 1) * ROWS, :] = new
         d_ref[at, :] = fresh
+
+    def step(i, carry):
+        if beside is not None:
+            beside(i)
+        panel(2 * i)
+        panel(2 * i + 1)
         return carry
 
-    lax.fori_loop(0, panels, step, 0)
+    lax.fori_loop(0, panels // 2, step, 0)
 
 
 def band_width(width):
@@ -114,12 +120,6 @@
     pair.wait()
     turned[:, :half] = stacked_ref[:, pl.ds(pl.multiple_of(c * half, half), half)]
     turned[:, half:] = stacked_ref[:, pl.ds(pl.multiple_of(other * half, half), half)]
-    for i in range(half // SIDE):
-        lo = i * SIDE
-        part[lo : lo + SIDE, :] = dot(
-            turned[:, lo : lo + SIDE], turned[:, lo : lo + wide], ((0,), (0,))
-        )
-
     def shares(d):
         to, _ = away(d)
         return push(
@@ -127,8 +127,19 @@
             slots.at[d], sems.at[0, d], sems.at[1, d], to, c,
         )
 
-    for d in range(1, teams):
-        shares(d).start()
+    for i in range(half // SIDE):
+        lo = i * SIDE
+        part[lo : lo + SIDE, :] = dot(
+            turned[:, lo : lo + SIDE], turned[:, lo : lo + wide], ((0,), (0,))
+        )
+        for to in range(teams):
+            if ((to + 1) * rows - 1) // SIDE == i:
+                d = lax.rem(to - t + teams, teams)
+
+                @pl.when(d != 0)
+                def _():
+                    shares(d).start()
+
     total = part[pl.ds(pl.multiple_of(t * rows, rows), rows), :]
     for d in range(1, teams):
         shares(d).wait_recv()
@@ -190,7 +201,7 @@
     )(train_grads)
 
 
-def factor_kernel(band_ref, a_ref, inv_ref):
+def inverse_kernel(band_ref, a_ref, inv_ref, w_ref):
     width = band_ref.shape[0]
     count = width // SIDE
     eye = lax.broadcasted_iota(jnp.int32, (SIDE, SIDE), 0) == lax.broadcasted_iota(
@@ -206,70 +217,57 @@
             block = band_ref[span[i], span[d]]
             j = (i + d) % count
             if d == 0:
-                a_ref[span[i], span[i]] = block + jnp.where(eye, shift, 0.0)
-            elif j > i:
-                a_ref[span[i], span[j]] = block
-            elif 2 * d < count:
+                block = block + jnp.where(eye, shift, 0.0)
+            a_ref[span[i], span[j]] = block
+            if 0 < d and 2 * d < count:
                 a_ref[span[j], span[i]] = block.T
+
+    def update(k, slot, i):
+        at = pl.ds(pl.multiple_of(i * SIDE, SIDE), SIDE)
+        old = a_ref[at, :]
+        change = dot(old[:, span[k]], w_ref[slot])
+        a_ref[at, :] = old - change
+        a_ref[at, span[k]] = -change[:, span[k]]
+
+    inv_ref[...] = a_ref[span[0], span[0]]
+    invert_block(inv_ref)
     for k in range(count):
-        inv_ref[k] = a_ref[span[k], span[k]]
-        invert_block(inv_ref.at[k])
-        if k + 1 == count:
-            break
-        rest = a_ref[span[k], (k + 1) * SIDE :]
-        w = dot(inv_ref[k], rest)
-        for i in range(k + 1, count):
-            off = (i - k - 1) * SIDE
-            a_ref[span[i], i * SIDE :] -= dot(
-                rest[:, off : off + SIDE], w[:, off:], ((0,), (0,))
-            )
-        a_ref[span[k], (k + 1) * SIDE :] = w
-
-
-def solve_kernel(a_ref, inv_ref, query_ref, out_ref):
-    count = inv_ref.shape[0]
-    span = [slice(k * SIDE, (k + 1) * SIDE) for k in range(count)]
-    out_ref[...] = query_ref[...]
-    for k in range(count - 1):
-        out_ref[:, (k + 1) * SIDE :] -= dot(
-            out_ref[:, span[k]], a_ref[span[k], (k + 1) * SIDE :]
-        )
-    for k in reversed(range(count)):
-        z = dot(out_ref[:, span[k]], inv_ref[k])
+        slot = k % 2
+        w_ref[slot] = dot(inv_ref[...], a_ref[span[k], :])
+        w_ref[slot, :, span[k]] = inv_ref[...]
+        work = functools.partial(update, k, slot)
         if k + 1 < count:
-            z = z - dot(
-                out_ref[:, (k + 1) * SIDE :], a_ref[span[k], (k + 1) * SIDE :], ((1,), (1,))
-            )
-        out_ref[:, span[k]] = z
-
-
-def factor(band):
+            after = span[k + 1]
+            inv_ref[...] = a_ref[after, after] - dot(a_ref[after, span[k]], w_ref[slot, :, after])
+            steps = SIDE // (2 * ROWS)
+            each = -(-count // steps)
+            if each * steps == count:
+                invert_block(inv_ref, lambda i: [work(i * each + e) for e in range(each)])
+            else:
+                invert_block(inv_ref)
+                lax.fori_loop(0, count, lambda i, c: (work(i), c)[1], 0)
+        else:
+            lax.fori_loop(0, count, lambda i, c: (work(i), c)[1], 0)
+        a_ref[span[k], :] = w_ref[slot]
+
+
+def damped_inverse(band):
     width = band.shape[0]
     vmem = pl.BlockSpec(memory_space=pltpu.VMEM)
     return pl.pallas_call(
-        factor_kernel,
-        out_shape=[
-            jax.ShapeDtypeStruct((width, width), jnp.float32),
-            jax.ShapeDtypeStruct((width // SIDE, SIDE, SIDE), jnp.float32),
+        inverse_kernel,
+        out_shape=jax.ShapeDtypeStruct((width, width), jnp.float32),
+        in_specs=[vmem],
+        out_specs=vmem,
+        scratch_shapes=[
+            pltpu.VMEM((SIDE, SIDE), jnp.float32),
+            pltpu.VMEM((2, SIDE, width), jnp.float32),
         ],
-        in_specs=[vmem],
-        out_specs=[vmem, vmem],
         compiler_params=pltpu.CompilerParams(vmem_limit_bytes=48 * 2**20),
         cost_estimate=pl.CostEstimate(
             flops=12 * width**3, bytes_accessed=256 * 2**20, transcendentals=0
         ),
     )(band)
-
-
-def solve_rows(upper, inverses, queries):
-    vmem = pl.BlockSpec(memory_space=pltpu.VMEM)
-    return pl.pallas_call(
-        solve_kernel,
-        out_shape=jax.ShapeDtypeStruct(queries.shape, jnp.float32),
-        in_specs=[vmem, vmem, vmem],
-        out_specs=vmem,
-        compiler_params=pltpu.CompilerParams(vmem_limit_bytes=48 * 2**20),
-    )(upper, inverses, queries)
 
 
 def shards(train_grads, query_grads):
@@ -278,8 +276,8 @@
     stacked, band = gram_band(train_grads)
     band, query_grads = lax.optimization_barrier((band, query_grads))
     queries = lax.all_gather(query_grads, "train", axis=1, tiled=True)
-    upper, inverses = factor(band)
-    precond = solve_rows(upper, inverses, queries)
+    inverse = damped_inverse(band)
+    precond = jnp.dot(queries, inverse, preferred_element_type=jnp.float32, precision=HIGHEST)
     scores = jnp.dot(precond, stacked.T, preferred_element_type=jnp.float32, precision=HIGHEST)
     return scores * (count_docs / jnp.sqrt(jnp.float32(width)))
 

time: 184 us -> 175 us (0.951)
  the two profiles are of different devices: /device:TPU:29 before, /device:TPU:31 now
where the time goes in v3:
time: 175 us
  Pallas kernels  143 us (82%)
  matrix products  14.2 us (8%)
  between operations  13.4 us (8%)
  local copies, waits for them, and re-layouts  4.47 us (3%)
    pallas_call x1, Pallas kernels, damped_inverse(): pl.pallas_call(inverse_kernel, out_shape=jax.ShapeDtypeStruct((width, wid...  71.6 us
    pallas_call x1, Pallas kernels, gram_band(): pl.pallas_call(functools.partial(gram_kernel, teams), out_shape=[jax.Shap...  71 us
    dot_general x1, matrix products, shards(): jnp.dot(queries, inverse, preferred_element_type=jnp.float32, precision=H...  9.65 us
    dot_general x1, matrix products, shards(): jnp.dot(precond, stacked.T, preferred_element_type=jnp.float32, precision...  4.53 us
    unnamed x6, local copies, waits for them, and re-layouts  4.47 us
  transfers between devices with their start and end apart: 1, of which 0 were waited for; matrix products, arithmetic and copies ran while one was open for 0% of the time, Pallas kernels for 41%

profile of v3, /device:TPU:31, one launch (start us, length us, event | category | flops | bytes accessed | tf_op | source)
XLA Modules:
  0.0 174.7 jit_solution(12293769624731295852)
XLA Ops:
  6.5 0.0 all-gather.2.cloned.1.call-start
  6.5 0.0 copy-start
  6.5 1.2 copy-done
  7.8 71.0 %shard_map.28 = (f32[512,1024]{1,0:T(8,128)S(1)}, f32[1024,640]{1,0:T(8,128)S(1)}) custom-call(f32[256,1024]{1,0:T(8,128)S(1)} %copy-done), custom_call_target="tpu_custom_call" | custom-call | tf_op jit(solution)/shard_map/pallas_call | solution.py:183
  78.8 0.0 copy-start.1
  78.8 1.5 copy-done.1
  80.3 0.0 all-gather.2.cloned.1.call-update
  80.3 0.0 copy-start.2
  80.4 1.7 copy-done.2
  82.1 71.6 %shard_map.29 = f32[1024,1024]{1,0:T(8,128)} custom-call(f32[1024,640]{1,0:T(8,128)S(1)} %copy-done.2), custom_call_target="tpu_custom_call" | custom-call | flops 12884901888 | bytes 268435456 | tf_op jit(solution)/shard_map/pallas_call | solution.py:257
  153.7 0.0 all-gather.2.cloned.1.call-done
  153.7 9.7 %fusion = f32[512,1024]{1,0:T(8,128)S(1)} fusion(f32[512,1024]{1,0:T(8,128)} %all-gather.2.cloned.1.call-done, f32[1024,1024]{1,0:T(8,128)} %shard_map.29), kind=kOutput, calls=%fused_computation.1 | convolution fusion | flops 6442450944 | bytes 8388608 | tf_op jit(solution)/shard_map/dot_general | solution.py:280
  163.4 4.5 %convolution_multiply_fusion = f32[512,512]{1,0:T(8,128)} fusion(f32[512,1024]{1,0:T(8,128)S(1)} %fusion, f32[512,1024]{1,0:T(8,128)S(1)} %get-tuple-element.12), kind=kOutput, calls=%fused_computation | convolution fusion | flops 3221487616 | bytes 5242880 | tf_op jit(solution)/shard_map/dot_general | solution.py:281
Async XLA Ops:
  6.5 147.2 %all-gather.2.cloned.1.call-start = ((), (), s32[]{:S(2)}) async-start(), calls=%async_computation | async-start | bytes 2359296 | tf_op jit(solution)/shard_map/all_gather | solution.py:278
  6.5 1.2 copy-start
  78.8 1.5 copy-start.1
  80.3 1.7 copy-start.2
Sparse Core Ops, SparseCore 0:
  80.5 48.8 all-gather.1

commit v4 on v3

--- a/solution.py
+++ b/solution.py
@@ -18,18 +18,47 @@
     )
 
 
+def parts_of(x):
+    high = x.astype(jnp.bfloat16)
+    left = x - high.astype(jnp.float32)
+    mid = left.astype(jnp.bfloat16)
+    return high, mid, (left - mid.astype(jnp.float32)).astype(jnp.bfloat16)
+
+
+def left_parts(x):
+    high, mid, low = parts_of(x)
+    return jnp.concatenate([high, high, high, mid, mid, low], axis=1)
+
+
+def right_parts(x):
+    high, mid, low = parts_of(x)
+    return jnp.concatenate([high, mid, low, high, mid, high], axis=0)
+
+
+def tree(terms):
+    while len(terms) > 1:
+        terms = [a + b for a, b in zip(terms[::2], terms[1::2])]
+    return terms[0]
+
+
+def reciprocal(x):
+    r = pl.reciprocal(x, approx=True)
+    r = r * (2.0 - x * r)
+    return r * (2.0 - x * r)
+
+
 def invert_small(cols, row):
     for s in range(ROWS):
-        inv = 1.0 / jnp.broadcast_to(cols[s][s : s + 1], cols[s].shape)
+        inv = reciprocal(jnp.broadcast_to(cols[s][s : s + 1], cols[s].shape))
         here = row == s
-        pivot = cols[s]
+        scaled = cols[s] * inv
         out = []
         for j in range(ROWS):
             if j == s:
-                out.append(jnp.where(here, inv, -pivot * inv))
+                out.append(jnp.where(here, inv, -scaled))
             else:
-                r = jnp.broadcast_to(cols[j][s : s + 1], pivot.shape) * inv
-                out.append(jnp.where(here, r, cols[j] - pivot * r))
+                r = jnp.broadcast_to(cols[j][s : s + 1], scaled.shape)
+                out.append(jnp.where(here, r * inv, cols[j] - scaled * r))
         cols = out
     return cols
 
@@ -38,38 +67,28 @@
     return jnp.take_along_axis(block, jnp.full(block.shape, lane, jnp.int32), axis=1)
 
 
-def invert_block(d_ref, beside=None):
+def invert_block(d_ref, beside):
     panels = SIDE // ROWS
     row = lax.broadcasted_iota(jnp.int32, (ROWS, SIDE), 0)
     lane = lax.broadcasted_iota(jnp.int32, (ROWS, SIDE), 1)
-
-    def panel(g):
+    for g in range(panels):
+        beside(g)
         base = g * ROWS
-        at = pl.ds(pl.multiple_of(base, ROWS), ROWS)
-        own = d_ref[at, :]
+        blocks = [d_ref[i * ROWS : (i + 1) * ROWS, :] for i in range(panels)]
+        own = blocks[g]
         cols = invert_small([spread(own, base + s) for s in range(ROWS)], row)
         inside = (lane >= base) & (lane < base + ROWS)
         start = jnp.where(inside, jnp.where(lane - base == row, 1.0, 0.0), own)
-        fresh = cols[0] * jnp.broadcast_to(start[0:1], start.shape)
-        for s in range(1, ROWS):
-            fresh = fresh + cols[s] * jnp.broadcast_to(start[s : s + 1], start.shape)
-        wide = [jnp.broadcast_to(fresh[s : s + 1], fresh.shape) for s in range(ROWS)]
+        fresh = tree([cols[s] * jnp.broadcast_to(start[s : s + 1], own.shape) for s in range(ROWS)])
+        wide = [jnp.broadcast_to(fresh[s : s + 1], own.shape) for s in range(ROWS)]
         for i in range(panels):
-            block = d_ref[i * ROWS : (i + 1) * ROWS, :]
-            new = jnp.where(inside, 0.0, block)
-            for s in range(ROWS):
-                new = new - spread(block, base + s) * wide[s]
+            if i == g:
+                new = fresh
+            else:
+                new = jnp.where(inside, 0.0, blocks[i]) - tree(
+                    [spread(blocks[i], base + s) * wide[s] for s in range(ROWS)]
+                )
             d_ref[i * ROWS : (i + 1) * ROWS, :] = new
-        d_ref[at, :] = fresh
-
-    def step(i, carry):
-        if beside is not None:
-            beside(i)
-        panel(2 * i)
-        panel(2 * i + 1)
-        return carry
-
-    lax.fori_loop(0, panels // 2, step, 0)
 
 
 def band_width(width):
@@ -201,7 +220,7 @@
     )(train_grads)
 
 
-def inverse_kernel(band_ref, a_ref, inv_ref, w_ref):
+def inverse_kernel(band_ref, a_ref, inv_ref, w_ref, terms_ref):
     width = band_ref.shape[0]
     count = width // SIDE
     eye = lax.broadcasted_iota(jnp.int32, (SIDE, SIDE), 0) == lax.broadcasted_iota(
@@ -222,33 +241,55 @@
             if 0 < d and 2 * d < count:
                 a_ref[span[j], span[i]] = block.T
 
-    def update(k, slot, i):
-        at = pl.ds(pl.multiple_of(i * SIDE, SIDE), SIDE)
-        old = a_ref[at, :]
-        change = dot(old[:, span[k]], w_ref[slot])
-        a_ref[at, :] = old - change
-        a_ref[at, span[k]] = -change[:, span[k]]
-
+    def cut(k):
+        return pl.ds(pl.multiple_of(k * SIDE, SIDE), SIDE)
+
+    def update(i, k, ready):
+        rows, cols = cut(i), cut(k)
+        own = a_ref[rows, cols]
+        change = jnp.dot(left_parts(own), terms_ref[...], preferred_element_type=jnp.float32)
+        a_ref[rows, :] = a_ref[rows, :] - change
+        there = jnp.dot(
+            left_parts(own), terms_ref[:, cols], preferred_element_type=jnp.float32
+        )
+        a_ref[rows, cols] = jnp.where(ready, -there, own)
+
+    w_ref[...] = jnp.zeros_like(w_ref)
+    terms_ref[...] = jnp.zeros_like(terms_ref)
     inv_ref[...] = a_ref[span[0], span[0]]
-    invert_block(inv_ref)
-    for k in range(count):
-        slot = k % 2
-        w_ref[slot] = dot(inv_ref[...], a_ref[span[k], :])
-        w_ref[slot, :, span[k]] = inv_ref[...]
-        work = functools.partial(update, k, slot)
-        if k + 1 < count:
-            after = span[k + 1]
-            inv_ref[...] = a_ref[after, after] - dot(a_ref[after, span[k]], w_ref[slot, :, after])
-            steps = SIDE // (2 * ROWS)
-            each = -(-count // steps)
-            if each * steps == count:
-                invert_block(inv_ref, lambda i: [work(i * each + e) for e in range(each)])
-            else:
-                invert_block(inv_ref)
-                lax.fori_loop(0, count, lambda i, c: (work(i), c)[1], 0)
-        else:
-            lax.fori_loop(0, count, lambda i, c: (work(i), c)[1], 0)
-        a_ref[span[k], :] = w_ref[slot]
+    panels = SIDE // ROWS
+
+    def step(k, carry):
+        last = jnp.maximum(k - 1, 0)
+
+        def beside(g):
+            for i in range(g * count // panels, (g + 1) * count // panels):
+                update(i, last, k > 0)
+
+        invert_block(inv_ref, beside)
+
+        @pl.when(k > 0)
+        def _():
+            a_ref[cut(last), :] = w_ref[...]
+
+        inverse = inv_ref[...]
+        w_ref[...] = jnp.dot(
+            left_parts(inverse), right_parts(a_ref[cut(k), :]), preferred_element_type=jnp.float32
+        )
+        w_ref[:, cut(k)] = inverse
+        terms_ref[...] = right_parts(w_ref[...])
+        after = cut(jnp.minimum(k + 1, count - 1))
+        inv_ref[...] = a_ref[after, after] - jnp.dot(
+            left_parts(a_ref[after, cut(k)]),
+            terms_ref[:, after],
+            preferred_element_type=jnp.float32,
+        )
+        return carry
+
+    lax.fori_loop(0, count, step, 0)
+    for i in range(count - 1):
+        update(i, count - 1, True)
+    a_ref[span[count - 1], :] = w_ref[...]
 
 
 def damped_inverse(band):
@@ -261,7 +302,8 @@
         out_specs=vmem,
         scratch_shapes=[
             pltpu.VMEM((SIDE, SIDE), jnp.float32),
-            pltpu.VMEM((2, SIDE, width), jnp.float32),
+            pltpu.VMEM((SIDE, width), jnp.float32),
+            pltpu.VMEM((6 * SIDE, width), jnp.bfloat16),
         ],
         compiler_params=pltpu.CompilerParams(vmem_limit_bytes=48 * 2**20),
         cost_estimate=pl.CostEstimate(

time: 175 us -> 155 us (0.89)
  the two profiles are of different devices: /device:TPU:31 before, /device:TPU:0 now
where the time goes in v4:
time: 155 us
  Pallas kernels  108 us (70%)
  matrix products  14.4 us (9%)
  waiting for transfers between devices  14.3 us (9%)
  between operations  13.4 us (9%)
  local copies, waits for them, and re-layouts  4.47 us (3%)
    pallas_call x1, Pallas kernels, gram_band(): pl.pallas_call(functools.partial(gram_kernel, teams), out_shape=[jax.Shap...  59.7 us
    pallas_call x1, Pallas kernels, damped_inverse(): pl.pallas_call(inverse_kernel, out_shape=jax.ShapeDtypeStruct((width, wid...  48.6 us
    all_gather x1, waiting for transfers between devices, shards(): queries = lax.all_gather(query_grads, 'train', axis=1, tiled=True)  14.3 us
    dot_general x1, matrix products, shards(): jnp.dot(queries, inverse, preferred_element_type=jnp.float32, precision=H...  9.87 us
    dot_general x1, matrix products, shards(): jnp.dot(precond, stacked.T, preferred_element_type=jnp.float32, precision...  4.53 us
    unnamed x6, local copies, waits for them, and re-layouts  4.47 us
  transfers between devices with their start and end apart: 1, of which 1 were waited for; matrix products, arithmetic and copies ran while one was open for 0% of the time, Pallas kernels for 31%

profile of v4, /device:TPU:0, one launch (start us, length us, event | category | flops | bytes accessed | tf_op | source)
XLA Modules:
  0.0 155.0 jit_solution(335976763034987382)
XLA Ops:
  6.5 0.0 all-gather.2.cloned.1.call-start
  6.5 0.0 copy-start
  6.5 1.2 copy-done
  7.8 59.7 %shard_map.28 = (f32[512,1024]{1,0:T(8,128)S(1)}, f32[1024,640]{1,0:T(8,128)S(1)}) custom-call(f32[256,1024]{1,0:T(8,128)S(1)} %copy-done), custom_call_target="tpu_custom_call" | custom-call | tf_op jit(solution)/shard_map/pallas_call | solution.py:202
  67.5 0.0 copy-start.1
  67.5 1.5 copy-done.1
  69.0 0.0 all-gather.2.cloned.1.call-update
  69.1 0.0 copy-start.2
  69.1 1.7 %copy-done.2 = f32[1024,640]{1,0:T(8,128)S(1)} copy-done((f32[1024,640]{1,0:T(8,128)S(1)}, f32[1024,640]{1,0:T(8,128)}, u32[]{:S(2)}) %copy-start.2) | copy-done | bytes 2621464
  70.8 48.6 %shard_map.29 = f32[1024,1024]{1,0:T(8,128)} custom-call(f32[1024,640]{1,0:T(8,128)S(1)} %copy-done.2), custom_call_target="tpu_custom_call" | custom-call | flops 12884901888 | bytes 268435456 | tf_op jit(solution)/shard_map/pallas_call | solution.py:298
  119.4 14.3 %all-gather.2.cloned.1.call-done = f32[512,1024]{1,0:T(8,128)} async-done(((f32[512,128]{1,0:T(8,128)}), f32[512,1024]{1,0:T(8,128)}) %all-gather.2.cloned.1.call-update) | async-done | bytes 2097168 | tf_op jit(solution)/shard_map/all_gather | solution.py:320
  133.8 9.9 %fusion = f32[512,1024]{1,0:T(8,128)S(1)} fusion(f32[512,1024]{1,0:T(8,128)} %all-gather.2.cloned.1.call-done, f32[1024,1024]{1,0:T(8,128)} %shard_map.29), kind=kOutput, calls=%fused_computation.1 | convolution fusion | flops 6442450944 | bytes 8388608 | tf_op jit(solution)/shard_map/dot_general | solution.py:322
  143.6 4.5 %convolution_multiply_fusion = f32[512,512]{1,0:T(8,128)} fusion(f32[512,1024]{1,0:T(8,128)S(1)} %fusion, f32[512,1024]{1,0:T(8,128)S(1)} %get-tuple-element.12), kind=kOutput, calls=%fused_computation | convolution fusion | flops 3221487616 | bytes 5242880 | tf_op jit(solution)/shard_map/dot_general | solution.py:323
Async XLA Ops:
  6.5 127.2 %all-gather.2.cloned.1.call-start = ((), (), s32[]{:S(2)}) async-start(), calls=%async_computation | async-start | bytes 2359296 | tf_op jit(solution)/shard_map/all_gather | solution.py:320
  6.5 1.2 copy-start
  67.5 1.5 copy-start.1
  69.1 1.7 %copy-start.2 = (f32[1024,640]{1,0:T(8,128)S(1)}, f32[1024,640]{1,0:T(8,128)}, u32[]{:S(2)}) copy-start(f32[1024,640]{1,0:T(8,128)} %copy-done.1) | copy-start | bytes 7864324
Sparse Core Ops, SparseCore 0:
  69.2 64.5 all-gather.1

commit v5 on v4

--- a/solution.py
+++ b/solution.py
@@ -95,18 +95,27 @@
     return width // 2 + SIDE
 
 
-def gram_kernel(teams, own_ref, stacked_ref, band_ref, turned, part, slots, sems, pair_sem):
+def gram_kernel(teams, own_ref, stacked_ref, band_ref, turned, part, near, far, sems, core_sems, pair_sem):
     docs, width = own_ref.shape
     half, wide = width // 2, band_width(width)
     rows = half // teams
+    pairs = teams // 2
     t, c = lax.axis_index("train"), lax.axis_index("query")
     other = 1 - c
-
-    def mine(team, core):
-        return pl.ds(pl.multiple_of(core * half + team * rows, rows), rows)
-
-    def away(d):
-        return lax.rem(t + d, teams), lax.rem(t + teams - d, teams)
+    u, y = t // 2, t % 2
+    mate = t + 1 - 2 * y
+
+    def ahead(d):
+        return (u + d) % pairs
+
+    def behind(d):
+        return (u + pairs - d) % pairs
+
+    def mine(team):
+        return pl.ds(pl.multiple_of(c * half + team * rows, rows), rows)
+
+    def share(team):
+        return pl.ds(pl.multiple_of(team * rows, rows), rows)
 
     def push(src, dst, send, recv, team, core):
         return pltpu.make_async_remote_copy(
@@ -119,16 +128,12 @@
         )
 
     barrier = pltpu.get_barrier_semaphore()
-    for d in range(1, teams):
+    for team, core in [(2 * ahead(d) + y, c) for d in range(1, pairs)] + [(mate, c), (t, other)]:
         pl.semaphore_signal(
-            barrier, inc=1, device_id={"train": away(d)[0], "query": c},
+            barrier, inc=1, device_id={"train": team, "query": core},
             device_id_type=pl.DeviceIdType.MESH,
         )
-    pl.semaphore_signal(
-        barrier, inc=1, device_id={"train": t, "query": other},
-        device_id_type=pl.DeviceIdType.MESH,
-    )
-    pl.semaphore_wait(barrier, teams)
+    pl.semaphore_wait(barrier, pairs + 1)
 
     def docs_of(core):
         return pl.ds(pl.multiple_of(core * docs, docs), docs)
@@ -139,11 +144,16 @@
     pair.wait()
     turned[:, :half] = stacked_ref[:, pl.ds(pl.multiple_of(c * half, half), half)]
     turned[:, half:] = stacked_ref[:, pl.ds(pl.multiple_of(other * half, half), half)]
-    def shares(d):
-        to, _ = away(d)
+
+    def to_mate(v):
         return push(
-            part.at[pl.ds(pl.multiple_of(to * rows, rows), rows), :],
-            slots.at[d], sems.at[0, d], sems.at[1, d], to, c,
+            part.at[share(2 * v + 1 - y), :], near.at[v], sems.at[0, v], sems.at[1, v], mate, c
+        )
+
+    def to_owner(d):
+        team = 2 * ahead(d) + y
+        return push(
+            part.at[share(team), :], far.at[d], sems.at[2, d], sems.at[3, d], team, c
         )
 
     for i in range(half // SIDE):
@@ -151,46 +161,57 @@
         part[lo : lo + SIDE, :] = dot(
             turned[:, lo : lo + SIDE], turned[:, lo : lo + wide], ((0,), (0,))
         )
-        for to in range(teams):
-            if ((to + 1) * rows - 1) // SIDE == i:
-                d = lax.rem(to - t + teams, teams)
-
-                @pl.when(d != 0)
-                def _():
-                    shares(d).start()
-
-    total = part[pl.ds(pl.multiple_of(t * rows, rows), rows), :]
-    for d in range(1, teams):
-        shares(d).wait_recv()
-        total = total + slots[d]
-    band_ref[mine(t, c), :] = total
-
-    def spreads(d):
+        for v in range(pairs):
+            if ((2 * v + 2) * rows - 1) // SIDE == i:
+                to_mate(v).start()
+    for d in range(1, pairs):
+        v = ahead(d)
+        to_mate(v).wait_recv()
+        part[share(2 * v + y), :] = part[share(2 * v + y), :] + near[v]
+        to_owner(d).start()
+    to_mate(u).wait_recv()
+    total = part[share(t), :] + near[u]
+    for d in range(1, pairs):
+        to_owner(d).wait_recv()
+        total = total + far[d]
+    band_ref[mine(t), :] = total
+
+    def spread_far(d):
+        piece = band_ref.at[mine(t), :]
+        return push(piece, piece, sems.at[4, d], sems.at[5, d], 2 * ahead(d) + y, c)
+
+    def spread_near(d):
+        piece = band_ref.at[mine(2 * behind(d) + y), :]
+        return push(piece, piece, sems.at[6, d], sems.at[7, d], mate, c)
+
+    def spread_core(d, q):
+        piece = band_ref.at[mine(2 * behind(d) + (y if q == 0 else 1 - y)), :]
         return push(
-            band_ref.at[mine(t, c), :], band_ref.at[mine(t, c), :],
-            sems.at[2, d], sems.at[3, d], away(d)[0], c,
-        )
-
-    def relays(d):
-        owner = away(d)[1]
-        return push(
-            band_ref.at[mine(owner, c), :], band_ref.at[mine(owner, c), :],
-            sems.at[4, d], sems.at[5, d], t, other,
-        )
-
-    for d in range(1, teams):
-        spreads(d).start()
-    relays(0).start()
-    for d in range(1, teams):
-        spreads(d).wait_recv()
-        relays(d).start()
-    for d in range(teams):
-        relays(d).wait_recv()
-    for d in range(1, teams):
-        shares(d).wait_send()
-        spreads(d).wait_send()
-    for d in range(teams):
-        relays(d).wait_send()
+            piece, piece, core_sems.at[0, 2 * d + q], core_sems.at[1, 2 * d + q], t, other
+        )
+
+    for d in range(1, pairs):
+        spread_far(d).start()
+    spread_near(0).start()
+    spread_core(0, 0).start()
+    for d in range(1, pairs):
+        spread_far(d).wait_recv()
+        spread_near(d).start()
+        spread_core(d, 0).start()
+    for d in range(pairs):
+        spread_near(d).wait_recv()
+        spread_core(d, 1).start()
+    for d in range(pairs):
+        spread_core(d, 0).wait_recv()
+        spread_core(d, 1).wait_recv()
+    for d in range(pairs):
+        to_mate(d).wait_send()
+        spread_near(d).wait_send()
+        spread_core(d, 0).wait_send()
+        spread_core(d, 1).wait_send()
+        if d:
+            to_owner(d).wait_send()
+            spread_far(d).wait_send()
 
 
 def gram_band(train_grads):
@@ -210,8 +231,10 @@
         scratch_shapes=[
             pltpu.VMEM((2 * docs, width), jnp.float32),
             pltpu.VMEM((width // 2, wide), jnp.float32),
-            pltpu.VMEM((teams, rows, wide), jnp.float32),
-            pltpu.SemaphoreType.DMA((6, teams)),
+            pltpu.VMEM((teams // 2, rows, wide), jnp.float32),
+            pltpu.VMEM((teams // 2, rows, wide), jnp.float32),
+            pltpu.SemaphoreType.DMA((8, teams // 2)),
+            pltpu.SemaphoreType.DMA((2, teams)),
             pltpu.SemaphoreType.DMA((2,)),
         ],
         compiler_params=pltpu.CompilerParams(

time: 155 us -> 142 us (0.916)
  waiting for transfers between devices: 14.3 us -> 6.43 us
  Pallas kernels: 108 us -> 103 us
    all_gather x1, waiting for transfers between devices: 14.3 us -> 6.41 us  [shards(): queries = lax.all_gather(query_grads, 'train', axis=1, tiled=True)]
    pallas_call x1, Pallas kernels: 59.7 us -> 54.7 us  [gram_band(): pl.pallas_call(functools.partial(gram_kernel, teams), out_shape=[jax.Shap...]
  transfers between devices with their start and end apart: 1 -> 1, of which waited for: 1 -> 1; matrix products, arithmetic and copies ran while one was open for 0% -> 0% of each run, Pallas kernels for 31% -> 34%
where the time goes in v5:
time: 142 us
  Pallas kernels  103 us (73%)
  matrix products  14.4 us (10%)
  between operations  13.4 us (9%)
  waiting for transfers between devices  6.43 us (5%)
  local copies, waits for them, and re-layouts  4.47 us (3%)
    pallas_call x1, Pallas kernels, gram_band(): pl.pallas_call(functools.partial(gram_kernel, teams), out_shape=[jax.Shap...  54.7 us
    pallas_call x1, Pallas kernels, damped_inverse(): pl.pallas_call(inverse_kernel, out_shape=jax.ShapeDtypeStruct((width, wid...  48.6 us
    dot_general x1, matrix products, shards(): jnp.dot(queries, inverse, preferred_element_type=jnp.float32, precision=H...  9.87 us
    all_gather x1, waiting for transfers between devices, shards(): queries = lax.all_gather(query_grads, 'train', axis=1, tiled=True)  6.41 us
    dot_general x1, matrix products, shards(): jnp.dot(precond, stacked.T, preferred_element_type=jnp.float32, precision...  4.53 us
    unnamed x6, local copies, waits for them, and re-layouts  4.47 us
  transfers between devices with their start and end apart: 1, of which 1 were waited for; matrix products, arithmetic and copies ran while one was open for 0% of the time, Pallas kernels for 34%

profile of v5, /device:TPU:0, one launch (start us, length us, event | category | flops | bytes accessed | tf_op | source)
XLA Modules:
  0.0 142.1 jit_solution(17288341552364725766)
XLA Ops:
  6.5 0.0 all-gather.2.cloned.1.call-start
  6.5 0.0 copy-start
  6.5 1.2 copy-done
  7.8 54.7 %shard_map.28 = (f32[512,1024]{1,0:T(8,128)S(1)}, f32[1024,640]{1,0:T(8,128)S(1)}) custom-call(f32[256,1024]{1,0:T(8,128)S(1)} %copy-done), custom_call_target="tpu_custom_call" | custom-call | tf_op jit(solution)/shard_map/pallas_call | solution.py:223
  62.5 0.0 copy-start.1
  62.5 1.5 %copy-done.1 = f32[1024,640]{1,0:T(8,128)} copy-done((f32[1024,640]{1,0:T(8,128)}, f32[1024,640]{1,0:T(8,128)S(1)}, u32[]{:S(2)}) %copy-start.1) | copy-done | bytes 2621464
  64.0 0.0 all-gather.2.cloned.1.call-update
  64.0 0.0 copy-start.2
  64.0 1.7 %copy-done.2 = f32[1024,640]{1,0:T(8,128)S(1)} copy-done((f32[1024,640]{1,0:T(8,128)S(1)}, f32[1024,640]{1,0:T(8,128)}, u32[]{:S(2)}) %copy-start.2) | copy-done | bytes 2621464
  65.8 48.6 %shard_map.29 = f32[1024,1024]{1,0:T(8,128)} custom-call(f32[1024,640]{1,0:T(8,128)S(1)} %copy-done.2), custom_call_target="tpu_custom_call" | custom-call | flops 12884901888 | bytes 268435456 | tf_op jit(solution)/shard_map/pallas_call | solution.py:321
  114.4 6.4 %all-gather.2.cloned.1.call-done = f32[512,1024]{1,0:T(8,128)} async-done(((f32[512,128]{1,0:T(8,128)}), f32[512,1024]{1,0:T(8,128)}) %all-gather.2.cloned.1.call-update) | async-done | bytes 2097168 | tf_op jit(solution)/shard_map/all_gather | solution.py:343
  120.8 9.9 %fusion = f32[512,1024]{1,0:T(8,128)S(1)} fusion(f32[512,1024]{1,0:T(8,128)} %all-gather.2.cloned.1.call-done, f32[1024,1024]{1,0:T(8,128)} %shard_map.29), kind=kOutput, calls=%fused_computation.1 | convolution fusion | flops 6442450944 | bytes 8388608 | tf_op jit(solution)/shard_map/dot_general | solution.py:345
  130.7 4.5 %convolution_multiply_fusion = f32[512,512]{1,0:T(8,128)} fusion(f32[512,1024]{1,0:T(8,128)S(1)} %fusion, f32[512,1024]{1,0:T(8,128)S(1)} %get-tuple-element.12), kind=kOutput, calls=%fused_computation | convolution fusion | flops 3221487616 | bytes 5242880 | tf_op jit(solution)/shard_map/dot_general | solution.py:346
Async XLA Ops:
  6.5 114.3 %all-gather.2.cloned.1.call-start = ((), (), s32[]{:S(2)}) async-start(), calls=%async_computation | async-start | bytes 2359296 | tf_op jit(solution)/shard_map/all_gather | solution.py:343
  6.5 1.2 copy-start
  62.5 1.5 %copy-start.1 = (f32[1024,640]{1,0:T(8,128)}, f32[1024,640]{1,0:T(8,128)S(1)}, u32[]{:S(2)}) copy-start(f32[1024,640]{1,0:T(8,128)S(1)} %get-tuple-element.11.band_ref) | copy-start | bytes 7864324
  64.0 1.7 %copy-start.2 = (f32[1024,640]{1,0:T(8,128)S(1)}, f32[1024,640]{1,0:T(8,128)}, u32[]{:S(2)}) copy-start(f32[1024,640]{1,0:T(8,128)} %copy-done.1) | copy-start | bytes 7864324
Sparse Core Ops, SparseCore 0:
  64.2 56.6 all-gather.1

commit v6 on v5

--- a/solution.py
+++ b/solution.py
@@ -141,9 +141,21 @@
     pair = push(own_ref, stacked_ref.at[docs_of(c), :], pair_sem.at[0], pair_sem.at[1], t, other)
     pair.start()
     stacked_ref[docs_of(c), :] = own_ref[...]
+
+    def turn(core):
+        at = docs_of(core)
+        turned[at, :half] = stacked_ref[at, pl.ds(pl.multiple_of(c * half, half), half)]
+        turned[at, half:] = stacked_ref[at, pl.ds(pl.multiple_of(other * half, half), half)]
+
+    def product(core, lo):
+        at = docs_of(core)
+        return dot(turned[at, lo : lo + SIDE], turned[at, lo : lo + wide], ((0,), (0,)))
+
+    turn(c)
+    for i in range(half // SIDE):
+        part[i * SIDE : (i + 1) * SIDE, :] = product(c, i * SIDE)
     pair.wait()
-    turned[:, :half] = stacked_ref[:, pl.ds(pl.multiple_of(c * half, half), half)]
-    turned[:, half:] = stacked_ref[:, pl.ds(pl.multiple_of(other * half, half), half)]
+    turn(other)
 
     def to_mate(v):
         return push(
@@ -158,9 +170,7 @@
 
     for i in range(half // SIDE):
         lo = i * SIDE
-        part[lo : lo + SIDE, :] = dot(
-            turned[:, lo : lo + SIDE], turned[:, lo : lo + wide], ((0,), (0,))
-        )
+        part[lo : lo + SIDE, :] += product(other, lo)
         for v in range(pairs):
             if ((2 * v + 2) * rows - 1) // SIDE == i:
                 to_mate(v).start()

time: 142 us -> 141 us (level)
  no operation moved by 1% of the time
where the time goes in v6:
time: 141 us
  Pallas kernels  103 us (73%)
  matrix products  14.4 us (10%)
  between operations  13.4 us (10%)
  waiting for transfers between devices  6.44 us (5%)
  local copies, waits for them, and re-layouts  4.47 us (3%)
    pallas_call x1, Pallas kernels, gram_band(): pl.pallas_call(functools.partial(gram_kernel, teams), out_shape=[jax.Shap...  53.9 us
    pallas_call x1, Pallas kernels, damped_inverse(): pl.pallas_call(inverse_kernel, out_shape=jax.ShapeDtypeStruct((width, wid...  48.6 us
    dot_general x1, matrix products, shards(): jnp.dot(queries, inverse, preferred_element_type=jnp.float32, precision=H...  9.87 us
    all_gather x1, waiting for transfers between devices, shards(): queries = lax.all_gather(query_grads, 'train', axis=1, tiled=True)  6.43 us
    dot_general x1, matrix products, shards(): jnp.dot(precond, stacked.T, preferred_element_type=jnp.float32, precision...  4.53 us
    unnamed x6, local copies, waits for them, and re-layouts  4.47 us
  transfers between devices with their start and end apart: 1, of which 1 were waited for; matrix products, arithmetic and copies ran while one was open for 0% of the time, Pallas kernels for 34%

profile of v6, /device:TPU:0, one launch (start us, length us, event | category | flops | bytes accessed | tf_op | source)
XLA Modules:
  0.0 141.3 jit_solution(851436757459585839)
XLA Ops:
  6.5 0.0 all-gather.2.cloned.1.call-start
  6.5 0.0 copy-start
  6.5 1.2 copy-done
  7.8 53.9 %shard_map.28 = (f32[512,1024]{1,0:T(8,128)S(1)}, f32[1024,640]{1,0:T(8,128)S(1)}) custom-call(f32[256,1024]{1,0:T(8,128)S(1)} %copy-done), custom_call_target="tpu_custom_call" | custom-call | tf_op jit(solution)/shard_map/pallas_call | solution.py:233
  61.7 0.0 copy-start.1
  61.7 1.5 %copy-done.1 = f32[1024,640]{1,0:T(8,128)} copy-done((f32[1024,640]{1,0:T(8,128)}, f32[1024,640]{1,0:T(8,128)S(1)}, u32[]{:S(2)}) %copy-start.1) | copy-done | bytes 2621464
  63.2 0.0 all-gather.2.cloned.1.call-update
  63.3 0.0 copy-start.2
  63.3 1.7 %copy-done.2 = f32[1024,640]{1,0:T(8,128)S(1)} copy-done((f32[1024,640]{1,0:T(8,128)S(1)}, f32[1024,640]{1,0:T(8,128)}, u32[]{:S(2)}) %copy-start.2) | copy-done | bytes 2621464
  65.0 48.6 %shard_map.29 = f32[1024,1024]{1,0:T(8,128)} custom-call(f32[1024,640]{1,0:T(8,128)S(1)} %copy-done.2), custom_call_target="tpu_custom_call" | custom-call | flops 12884901888 | bytes 268435456 | tf_op jit(solution)/shard_map/pallas_call | solution.py:331
  113.6 6.4 %all-gather.2.cloned.1.call-done = f32[512,1024]{1,0:T(8,128)} async-done(((f32[512,128]{1,0:T(8,128)}), f32[512,1024]{1,0:T(8,128)}) %all-gather.2.cloned.1.call-update) | async-done | bytes 2097168 | tf_op jit(solution)/shard_map/all_gather | solution.py:353
  120.1 9.9 %fusion = f32[512,1024]{1,0:T(8,128)S(1)} fusion(f32[512,1024]{1,0:T(8,128)} %all-gather.2.cloned.1.call-done, f32[1024,1024]{1,0:T(8,128)} %shard_map.29), kind=kOutput, calls=%fused_computation.1 | convolution fusion | flops 6442450944 | bytes 8388608 | tf_op jit(solution)/shard_map/dot_general | solution.py:355
  129.9 4.5 %convolution_multiply_fusion = f32[512,512]{1,0:T(8,128)} fusion(f32[512,1024]{1,0:T(8,128)S(1)} %fusion, f32[512,1024]{1,0:T(8,128)S(1)} %get-tuple-element.12), kind=kOutput, calls=%fused_computation | convolution fusion | flops 3221487616 | bytes 5242880 | tf_op jit(solution)/shard_map/dot_general | solution.py:356
Async XLA Ops:
  6.5 113.5 %all-gather.2.cloned.1.call-start = ((), (), s32[]{:S(2)}) async-start(), calls=%async_computation | async-start | bytes 2359296 | tf_op jit(solution)/shard_map/all_gather | solution.py:353
  6.5 1.2 copy-start
  61.7 1.5 %copy-start.1 = (f32[1024,640]{1,0:T(8,128)}, f32[1024,640]{1,0:T(8,128)S(1)}, u32[]{:S(2)}) copy-start(f32[1024,640]{1,0:T(8,128)S(1)} %get-tuple-element.11.band_ref) | copy-start | bytes 7864324
  63.3 1.7 %copy-start.2 = (f32[1024,640]{1,0:T(8,128)S(1)}, f32[1024,640]{1,0:T(8,128)}, u32[]{:S(2)}) copy-start(f32[1024,640]{1,0:T(8,128)} %copy-done.1) | copy-start | bytes 7864324
Sparse Core Ops, SparseCore 0:
  63.4 56.6 all-gather.1
